TPU v7x, 512 devices: a whole 4x4x16 slice. The times are simulated.
512 devices in a mesh: group: 32 (over z, core), tensor: 16 (over y, x).
Axes of the slice: x: 4, y: 4, z: 16, core: 2. Of those that a mesh axis runs over, the one named last changes fastest.
Arguments:
- queries: bfloat16 [384, 4, 8192], P('group', None, 'tensor'), may hold values from -603 to 603
- new_entries: bfloat16 [384, 4, 2048], P('group'), may hold values from -6 to 6
- resident_cache: bfloat16 [128, 512, 2048], P('group', 'tensor'), may hold values from -6 to 6
- prefill_cache: bfloat16 [256, 512, 2048], P('group', 'tensor'), may hold values from -6 to 6
- resident_kept: int32 [128], replicated, may hold values from 256 to 512, as said below
- kept_tokens: int32 [256], replicated, may hold values from 1 to 512, as said below
- prefill_slot: int32 [256], replicated, may hold values from 0 to 255, as said below
- decode_slot: int32 [256], replicated, may hold values from 4 to 383, as said below
Outputs:
- attended: bfloat16 [384, 4, 8192], P('group', None, 'tensor')
Inputs may be any that keep to these rules, and one draw needn't show every extreme that they name: `kept_tokens`: some request keeps exactly 512 positions. `prefill_slot`: A permutation of the 256 prefill slots; slot s lies in prefill group s // 8. `decode_slot`: every slot g * 12 + l with l >= 4 is named by exactly one request; from one prefill group to one decode group go at most 1 request, and exactly 1 for some pairs. `resident_kept`: some resident request keeps exactly 512 positions.
All inputs are finite; a program needn't handle non-finite values.
Results may differ from a plain program's by a relative error of at most 0.0044.
Values may be sent and summed in bfloat16 or wider, within the bound.
No kernel may reach another device: no remote copies, remote signals or barrier semaphores. Data moves between devices by JAX's collectives and lax.ppermute only.
A program may use at most 128 MiB of HBM per device.

v0:
```python
import math
import jax
import jax.numpy as jnp
from jax import lax
from jax.sharding import PartitionSpec as P

H = 64
KVH = 8
HD = 128
STEPS = 4
MIG_DEV = 8
RES_DEV = 4
NEG_FLOOR = -1e30


def combined_all(part, axis, combine):
    gathered = jax.tree.map(lambda a: lax.all_gather(a, axis), part)

    def take(source):
        return jax.tree.map(lambda a: lax.dynamic_index_in_dim(a, source, 0, False), gathered)

    return lax.fori_loop(
        1, lax.axis_size(axis), lambda source, state: combine(state, take(source)), take(0)
    )


def routing(kept_tokens, prefill_slot, decode_slot, groups, per_pair):
    slot_count = MIG_DEV * groups
    per_group = RES_DEV + MIG_DEV
    dest_by_slot = jnp.zeros((slot_count,), jnp.int32).at[prefill_slot].set(decode_slot)
    kept_by_slot = jnp.zeros((slot_count,), jnp.int32).at[prefill_slot].set(kept_tokens)
    dest_group = (dest_by_slot // per_group).reshape(groups, MIG_DEV)
    earlier = jnp.arange(MIG_DEV)[None, :] < jnp.arange(MIG_DEV)[:, None]
    matching = dest_group[:, :, None] == dest_group[:, None, :]
    ranking = jnp.sum((matching & earlier[None]).astype(jnp.int32), axis=2)
    outgoing_row = (dest_group * per_pair + ranking).reshape(slot_count)
    source_by_dslot = jnp.zeros((groups * per_group,), jnp.int32).at[decode_slot].set(prefill_slot)
    return (kept_by_slot, ranking.reshape(slot_count), outgoing_row, source_by_dslot)


def partials(asking, stored, lengths, offset):
    row_count = stored.shape[0]
    stride = stored.shape[1]
    sharing = H // KVH
    asked_rows = asking.reshape(row_count, STEPS, KVH, sharing, HD)
    entries = stored.reshape(row_count, stride, 2, KVH, HD)
    scores = jnp.einsum(
        "rtkgd,rpkd->rtkgp", asked_rows, entries[:, :, 0], preferred_element_type=jnp.float32
    ) * (1.0 / math.sqrt(HD))
    usable = (offset + jnp.arange(stride))[None, :] < lengths[:, None]
    usable = usable[:, None, None, None, :]
    highest = jnp.max(jnp.where(usable, scores, NEG_FLOOR), axis=4)
    weights = jnp.where(usable, jnp.exp(scores - highest[..., None]), 0.0)
    totals = jnp.sum(weights, axis=4)
    blended = jnp.einsum(
        "rtkgp,rpkd->rtkgd",
        weights.astype(jnp.bfloat16),
        entries[:, :, 1],
        preferred_element_type=jnp.float32,
    )
    return (
        highest.reshape(row_count, STEPS, H),
        totals.reshape(row_count, STEPS, H),
        blended.reshape(row_count, STEPS, H, HD),
    )


def combine(earlier, later):
    highest = jnp.maximum(earlier[0], later[0])
    first_factor = jnp.exp(earlier[0] - highest)
    second_factor = jnp.exp(later[0] - highest)
    return (
        highest,
        earlier[1] * first_factor + later[1] * second_factor,
        earlier[2] * first_factor[..., None] + later[2] * second_factor[..., None],
    )


def own_heads(parts):
    shards = lax.axis_size("tensor")
    stride_heads = H // shards
    merged = combined_all(parts, "tensor", combine)
    start_head = lax.axis_index("tensor") * stride_heads
    result = tuple(
        (lax.dynamic_slice_in_dim(member, start_head, stride_heads, 2) for member in merged)
    )
    return result


def body(
    queries,
    new_entries,
    resident_cache,
    prefill_cache,
    resident_kept,
    kept_tokens,
    prefill_slot,
    decode_slot,
):
    groups = lax.axis_size("group")
    shards = lax.axis_size("tensor")
    per_pair = max(1, MIG_DEV // groups)
    per_group = RES_DEV + MIG_DEV
    stride = prefill_cache.shape[1]
    features = prefill_cache.shape[2]
    offset = lax.axis_index("tensor") * stride
    group_here = lax.axis_index("group")
    kept_by_slot, ranking, outgoing_row, source_by_dslot = routing(
        kept_tokens, prefill_slot, decode_slot, groups, per_pair
    )
    local_rows = lax.dynamic_slice_in_dim(outgoing_row, group_here * MIG_DEV, MIG_DEV)
    arriving = lax.dynamic_slice_in_dim(source_by_dslot, group_here * per_group + RES_DEV, MIG_DEV)
    arriving_rows = arriving // MIG_DEV * per_pair + ranking[arriving]
    arriving_kept = kept_by_slot[arriving]
    resident_len = lax.dynamic_slice_in_dim(resident_kept, group_here * RES_DEV, RES_DEV)
    asking = lax.all_gather(queries, "tensor", axis=2, tiled=True)
    resident_parts = partials(asking[:RES_DEV], resident_cache, resident_len, offset)
    outgoing = (
        jnp.zeros((groups * per_pair, stride, features), jnp.bfloat16)
        .at[local_rows]
        .set(prefill_cache)
    )
    arrived = lax.all_to_all(
        outgoing.reshape(groups, per_pair, stride, features),
        "group",
        split_axis=0,
        concat_axis=0,
        tiled=True,
    )
    moved_cache = arrived.reshape(groups * per_pair, stride, features)[arriving_rows]
    moved_parts = partials(asking[RES_DEV:], moved_cache, arriving_kept, offset)
    heads_parts = own_heads(
        tuple(
            (
                jnp.concatenate([former, latter], 0)
                for former, latter in zip(resident_parts, moved_parts)
            )
        )
    )
    highest, totals, blended = heads_parts
    stride_heads = H // shards
    sharing = H // KVH
    heads_here = lax.axis_index("tensor") * stride_heads + jnp.arange(stride_heads)
    pairs_here = heads_here // sharing
    asked_here = queries.reshape(per_group, STEPS, stride_heads, HD)
    newest = new_entries.reshape(per_group, STEPS, 2, KVH, HD)
    new_keys = jnp.take(newest[:, :, 0], pairs_here, axis=2)
    new_values = jnp.take(newest[:, :, 1], pairs_here, axis=2)
    scores = jnp.einsum(
        "rthd,ruhd->rthu", asked_here, new_keys, preferred_element_type=jnp.float32
    ) * (1.0 / math.sqrt(HD))
    causal = (jnp.arange(STEPS)[None, :] <= jnp.arange(STEPS)[:, None])[None, :, None, :]
    new_high = jnp.max(jnp.where(causal, scores, NEG_FLOOR), axis=3)
    overall = jnp.maximum(highest, new_high)
    weights = jnp.where(causal, jnp.exp(scores - overall[..., None]), 0.0)
    carried = jnp.exp(highest - overall)
    totals = totals * carried + jnp.sum(weights, axis=3)
    blended = blended * carried[..., None] + jnp.einsum(
        "rthu,ruhd->rthd",
        weights.astype(jnp.bfloat16),
        new_values,
        preferred_element_type=jnp.float32,
    )
    return (
        (blended / totals[..., None])
        .astype(jnp.bfloat16)
        .reshape(per_group, STEPS, stride_heads * HD)
    )


def solution(mesh):
    in_specs = (
        P("group", None, "tensor"),
        P("group", None, None),
        P("group", "tensor", None),
        P("group", "tensor", None),
        P(),
        P(),
        P(),
        P(),
    )
    out_specs = P("group", None, "tensor")
    return jax.shard_map(body, mesh=mesh, in_specs=in_specs, out_specs=out_specs, check_vma=False)
```

profile of v0, /device:TPU:1, one launch (start us, length us, event | category | flops | bytes accessed | tf_op | source)
XLA Modules:
  0.0 440.8 jit_solution(7627150290861144147)
XLA Ops:
  6.5 0.7 compare_select_fusion
  7.2 1.6 scatter_custom_fusion.2
  9.3 2.5 broadcast_in_dim.118
  11.8 2.9 scatter_fusion
  14.7 16.9 %all-to-all-start = ((bf16[32,1,32,2048]{3,2,1,0:T(8,128)(2,1)}), bf16[32,1,32,2048]{3,2,1,0:T(8,128)(2,1)}, u32[]{:S(2)}, u32[]{:S(2)}) async-start(bf16[32,1,32,2048]{3,2,1,0:T(8,128)(2,1)} %bitcast.125), calls=%async_computation | async-start | bytes 8388608 | tf_op jit(solution)/shard_map/all_to_all | solution.py:123
  31.7 22.6 %all_gather.21 = bf16[12,4,8192]{2,1,0:T(4,128)(2,1)S(1)} all-gather(bf16[12,4,512]{2,1,0:T(4,128)(2,1)S(1)} %copy-done.4), channel_id=1, replica_groups=mesh['group'=32,'tensor'=16] {'tensor'}, dimensions={2}, use_global_device_ids=true | all-gather | bytes 835584 | tf_op jit(solution)/shard_map/all_gather | solution.py:116
  54.6 1.7 scatter_custom_fusion.1
  56.4 0.6 gather_fusion.1
  57.1 1.6 scatter_custom_fusion
  58.6 0.6 gather_fusion
  59.3 0.5 reshape.250
  60.5 0.4 select_reduce_fusion.1
  60.9 0.3 convolution_bitcast_fusion.1
  61.5 153.5 %all-to-all-done = bf16[32,1,32,2048]{3,2,1,0:T(8,128)(2,1)} async-done(((bf16[32,1,32,2048]{3,2,1,0:T(8,128)(2,1)}), bf16[32,1,32,2048]{3,2,1,0:T(8,128)(2,1)}, u32[]{:S(2)}, u32[]{:S(2)}) %all-to-all-start) | async-done | bytes 4194336 | tf_op jit(solution)/shard_map/all_to_all | solution.py:123
  214.9 2.8 gather_fusion.2
  218.2 0.5 select_reduce_fusion
  218.7 0.7 convolution_bitcast_fusion
  219.5 1.4 pad_maximum_fusion
  221.0 0.4 fusion.17
  222.1 0.6 gather_fusion.3
  222.7 0.6 gather_fusion.4
  223.4 0.7 select_bitcast_fusion
  224.7 0.8 fusion.10
  225.7 20.1 %all-gather.1 = f32[192,4,64]{2,1,0:T(4,128)S(1)} all-gather(f32[12,4,64]{2,1,0:T(4,128)S(1)} %copy.145), channel_id=3, replica_groups=mesh['group'=32,'tensor'=16] {'tensor'}, dimensions={0}, use_global_device_ids=true | all-gather | bytes 208896 | tf_op jit(solution)/shard_map/all_gather | solution.py:17
  245.9 21.4 %all-gather = f32[192,4,64]{2,1,0:T(4,128)S(1)} all-gather(f32[12,4,64]{2,1,0:T(4,128)S(1)} %pad_maximum_fusion.2), channel_id=2, replica_groups=mesh['group'=32,'tensor'=16] {'tensor'}, dimensions={0}, use_global_device_ids=true | all-gather | bytes 208896 | tf_op jit(solution)/shard_map/all_gather | solution.py:17
  267.3 124.1 %all-gather.5.cloned.1.call-done = f32[192,4,64,128]{3,2,1,0:T(8,128)} async-done(((f32[12,4,64,128]{3,2,1,0:T(8,128)}), f32[192,4,64,128]{3,2,1,0:T(8,128)}) %all-gather.5.cloned.1.call-update) | async-done | bytes 25165840 | tf_op jit(solution)/shard_map/all_gather | solution.py:17
  391.4 1.5 slice.56
  392.9 35.1 %while.19 = (s32[]{:T(128)}, f32[12,4,64]{2,1,0:T(4,128)S(1)}, f32[12,4,64]{2,1,0:T(4,128)S(1)}, f32[12,4,64,128]{3,2,1,0:T(8,128)S(1)}, f32[16,12,4,64]{3,2,1,0...) while((s32[]{:T(128)}, f32[12,4,64]{2,1,0:T(4,128)S(1)}, ...), condition=%wide.region_10.11_spmd, body=%wide.region_9.10_spmd.sunk | while | flops 1198085 | bytes 4841623 | solution.py:22
  393.0 2.3 fusion.49
  395.4 2.3 fusion.49
  397.7 2.3 fusion.49
  400.0 2.3 fusion.49
  402.4 2.3 fusion.49
  404.7 2.3 fusion.49
  407.1 2.3 fusion.49
  409.4 2.3 fusion.49
  411.7 2.3 fusion.49
  414.1 2.3 fusion.49
  416.4 2.3 fusion.49
  418.8 2.3 fusion.49
  421.1 2.3 fusion.49
  423.5 2.3 fusion.49
  425.8 2.3 fusion.49
  428.5 0.7 copy.172
  429.3 0.9 copy.161
  430.2 1.0 copy.150
  431.5 0.8 multiply_add_fusion
  432.3 1.6 fusion.8
  (84 shorter events, 5.3 us)
Async XLA Ops:
  9.3 2.5 copy-start
  14.7 17.0 %copy-start.4 = (bf16[12,4,512]{2,1,0:T(4,128)(2,1)S(1)}, bf16[12,4,512]{2,1,0:T(4,128)(2,1)}, u32[]{:S(2)}) copy-start(bf16[12,4,512]{2,1,0:T(4,128)(2,1)} %param.12) | copy-start | bytes 147460
  14.7 200.2 %all-to-all-start = ((bf16[32,1,32,2048]{3,2,1,0:T(8,128)(2,1)}), bf16[32,1,32,2048]{3,2,1,0:T(8,128)(2,1)}, u32[]{:S(2)}, u32[]{:S(2)}) async-start(bf16[32,1,32,2048]{3,2,1,0:T(8,128)(2,1)} %bitcast.125), calls=%async_computation | async-start | bytes 8388608 | tf_op jit(solution)/shard_map/all_to_all | solution.py:123
  31.7 359.8 %all-gather.5.cloned.1.call-start = ((), (), s32[]{:S(2)}) async-start(), calls=%async_computation.1 | async-start | bytes 26738688 | tf_op jit(solution)/shard_map/all_gather | solution.py:17
  54.5 5.6 %copy-start.1 = (bf16[4,32,2048]{2,1,0:T(8,128)(2,1)S(1)}, bf16[4,32,2048]{2,1,0:T(8,128)(2,1)}, u32[]{:S(2)}) copy-start(bf16[4,32,2048]{2,1,0:T(8,128)(2,1)} %param.14) | copy-start | bytes 1572868
  58.6 1.6 copy-start.5
  220.9 0.9 copy-start.3
  428.3 1.9 copy-start.2
Sparse Core Ops, SparseCore 0:
  221.1 170.3 all-gather.4
where the time goes:
time: 442 us; the launch traced here: 441 us
  waiting for transfers between devices  278 us (63%)
  blocking collectives  64.1 us (15%)
  other arithmetic  40.4 us (9%)
  local copies, waits for them, and re-layouts  23.7 us (5%)
  starting transfers between devices  17 us (4%)
  between operations  13.8 us (3%)
    all_to_all x1, waiting for transfers between devices, body(): lax.all_to_all(outgoing.reshape(groups, per_pair, stride, features), 'gro...  153 us
    all_gather x1, waiting for transfers between devices, combined_all(): gathered = jax.tree.map(lambda a: lax.all_gather(a, axis), part)  124 us
    all_gather x2, blocking collectives, combined_all(): gathered = jax.tree.map(lambda a: lax.all_gather(a, axis), part)  41.5 us
    add x15, other arithmetic, combine(): earlier[2] * first_factor[..., None] + later[2] * second_factor[..., None]  34 us
    all_gather x1, blocking collectives, body(): asking = lax.all_gather(queries, 'tensor', axis=2, tiled=True)  22.6 us
    all_to_all x1, starting transfers between devices, body(): lax.all_to_all(outgoing.reshape(groups, per_pair, stride, features), 'gro...  16.9 us
  transfers between devices with their start and end apart: 2, of which 2 were waited for; matrix products, arithmetic and copies ran while one was open for 3% of the time, Pallas kernels for 0%

commit v1 on v0

--- a/solution.py
+++ b/solution.py
@@ -11,6 +11,25 @@
 MIG_DEV = 8
 RES_DEV = 4
 NEG_FLOOR = -1e30
+
+
+def load_windows(panel):
+    axis_id = "tensor"
+    degree = jax.lax.axis_size(axis_id)
+    nodes = tuple(((idx, (idx + 1) % degree) for idx in range(degree)))
+    inbox = tuple(((idx, (idx - 1) % degree) for idx in range(degree)))
+    known, v_next = ([panel], [panel])
+    for _ in range(degree // 2):
+        work_now = jax.lax.ppermute(known[-1], axis_name=axis_id, perm=nodes)
+        known.append(work_now)
+    i = 0
+    while i < (degree - 1) // 2:
+        local_next = jax.lax.ppermute(v_next[-1], perm=inbox, axis_name=axis_id)
+        v_next.append(local_next)
+        i += 1
+    piece_next = jnp.concatenate([*known[::-1], *v_next[1:]], axis=2)
+    carry_in = jax.lax.axis_index(axis_id)
+    return jnp.roll(piece_next, (carry_in - degree // 2) * panel.shape[2], axis=2)
 
 
 def combined_all(part, axis, combine):
@@ -113,7 +132,7 @@
     arriving_rows = arriving // MIG_DEV * per_pair + ranking[arriving]
     arriving_kept = kept_by_slot[arriving]
     resident_len = lax.dynamic_slice_in_dim(resident_kept, group_here * RES_DEV, RES_DEV)
-    asking = lax.all_gather(queries, "tensor", axis=2, tiled=True)
+    asking = load_windows(queries)
     resident_parts = partials(asking[:RES_DEV], resident_cache, resident_len, offset)
     outgoing = (
         jnp.zeros((groups * per_pair, stride, features), jnp.bfloat16)

time: 442 us -> 442 us (level)
  starting transfers between devices: 17 us -> 79.3 us
  waiting for transfers between devices: 278 us -> 234 us
  blocking collectives: 64.1 us -> 41.2 us
    ppermute x0 -> x15, starting transfers between devices: none -> 62.3 us  [the longest x7 45.7 us: load_windows(): local_next = jax.lax.ppermute(v_next[-1], perm=inbox, axis_name=axis_id)]
    all_to_all x1, waiting for transfers between devices: 153 us -> 103 us  [body(): lax.all_to_all(outgoing.reshape(groups, per_pair, stride, features), 'gro...]
    all_gather x1 -> x0, blocking collectives: 22.6 us -> none  [body(): asking = lax.all_gather(queries, 'tensor', axis=2, tiled=True)]
    ppermute x0 -> x15, waiting for transfers between devices: none -> 7.25 us  [the longest x8 6.56 us: load_windows(): work_now = jax.lax.ppermute(known[-1], axis_name=axis_id, perm=nodes)]
  transfers between devices with their start and end apart: 2 -> 17, of which waited for: 2 -> 4; matrix products, arithmetic and copies ran while one was open for 3% -> 3% of each run, Pallas kernels for 0% -> 0%
where the time goes in v1:
time: 442 us; the launch traced here: 441 us
  waiting for transfers between devices  234 us (53%)
  starting transfers between devices  79.3 us (18%)
  blocking collectives  41.2 us (9%)
  other arithmetic  40.4 us (9%)
  local copies, waits for them, and re-layouts  27.3 us (6%)
  between operations  14.2 us (3%)
    all_gather x1, waiting for transfers between devices, combined_all(): gathered = jax.tree.map(lambda a: lax.all_gather(a, axis), part)  124 us
    all_to_all x1, waiting for transfers between devices, body(): lax.all_to_all(outgoing.reshape(groups, per_pair, stride, features), 'gro...  103 us
    ppermute x7, starting transfers between devices, load_windows(): local_next = jax.lax.ppermute(v_next[-1], perm=inbox, axis_name=axis_id)  45.7 us
    all_gather x2, blocking collectives, combined_all(): gathered = jax.tree.map(lambda a: lax.all_gather(a, axis), part)  41.2 us
    add x15, other arithmetic, combine(): earlier[2] * first_factor[..., None] + later[2] * second_factor[..., None]  34 us
    all_to_all x1, starting transfers between devices, body(): lax.all_to_all(outgoing.reshape(groups, per_pair, stride, features), 'gro...  17 us
    ppermute x8, starting transfers between devices, load_windows(): work_now = jax.lax.ppermute(known[-1], axis_name=axis_id, perm=nodes)  16.6 us
  transfers between devices with their start and end apart: 17, of which 4 were waited for; matrix products, arithmetic and copies ran while one was open for 3% of the time, Pallas kernels for 0%

profile of v1, /device:TPU:1, one launch (start us, length us, event | category | flops | bytes accessed | tf_op | source)
XLA Modules:
  0.0 440.8 jit_solution(11011536320553174350)
XLA Ops:
  7.2 1.6 scatter_custom_fusion.2
  9.3 2.5 broadcast_in_dim.118
  11.8 2.9 scatter_fusion
  14.7 17.0 %all-to-all-start = ((bf16[32,1,32,2048]{3,2,1,0:T(8,128)(2,1)}), bf16[32,1,32,2048]{3,2,1,0:T(8,128)(2,1)}, u32[]{:S(2)}, u32[]{:S(2)}) async-start(bf16[32,1,32,2048]{3,2,1,0:T(8,128)(2,1)} %bitcast.125), calls=%async_computation | async-start | bytes 8388608 | tf_op jit(solution)/shard_map/all_to_all | solution.py:142
  31.8 3.1 collective-permute-start
  34.9 5.6 %collective-permute-start.8 = (bf16[12,4,512]{2,1,0:T(4,128)(2,1)S(1)}, bf16[12,4,512]{2,1,0:T(4,128)(2,1)S(1)}, u32[]{:S(2)}, u32[]{:S(2)}) collective-permute-start(bf16[12,4,512]{2,1,0:T(4,128)(2,1)S(1)} %copy-done.3), channel_id=1, source_target_pairs={{0,15},{1,0},{2,1},{3,2},{4,3},{5,4},{6,5},{7,6},{8,7},{9,8},{10,9... | collective-permute-start | bytes 147464 | tf_op jit(solution)/shard_map/ppermute | solution.py:27
  40.8 1.6 scatter_custom_fusion.1
  42.4 1.9 collective-permute-start.1
  44.4 6.5 %collective-permute-done.1 = bf16[12,4,512]{2,1,0:T(4,128)(2,1)S(1)} collective-permute-done((bf16[12,4,512]{2,1,0:T(4,128)(2,1)S(1)}, bf16[12,4,512]{2,1,0:T(4,128)(2,1)S(1)}, u32[]{:S(2)}, u32[]{:S(2)}) %collective-permute-start.1) | collective-permute-done | bytes 49184 | tf_op jit(solution)/shard_map/ppermute | solution.py:23
  50.9 1.9 collective-permute-start.2
  52.9 6.7 %collective-permute-start.9 = (bf16[12,4,512]{2,1,0:T(4,128)(2,1)S(1)}, bf16[12,4,512]{2,1,0:T(4,128)(2,1)S(1)}, u32[]{:S(2)}, u32[]{:S(2)}) collective-permute-start(bf16[12,4,512]{2,1,0:T(4,128)(2,1)S(1)} %collective-permute-done.8), channel_id=1, source_target_pairs={{0,15},{1,0},{2,1},{3,2},{4,3},{5,4},{6,5},{7,6},{8,7},{9,8},{10,9... | collective-permute-start | bytes 147464 | tf_op jit(solution)/shard_map/ppermute | solution.py:27
  59.6 1.9 collective-permute-start.3
  61.5 1.6 scatter_custom_fusion
  63.7 6.7 %collective-permute-start.10 = (bf16[12,4,512]{2,1,0:T(4,128)(2,1)S(1)}, bf16[12,4,512]{2,1,0:T(4,128)(2,1)S(1)}, u32[]{:S(2)}, u32[]{:S(2)}) collective-permute-start(bf16[12,4,512]{2,1,0:T(4,128)(2,1)S(1)} %collective-permute-done.9), channel_id=1, source_target_pairs={{0,15},{1,0},{2,1},{3,2},{4,3},{5,4},{6,5},{7,6},{8,7},{9,8},{10,9... | collective-permute-start | bytes 147464 | tf_op jit(solution)/shard_map/ppermute | solution.py:27
  70.4 1.9 collective-permute-start.4
  72.5 6.7 %collective-permute-start.11 = (bf16[12,4,512]{2,1,0:T(4,128)(2,1)S(1)}, bf16[12,4,512]{2,1,0:T(4,128)(2,1)S(1)}, u32[]{:S(2)}, u32[]{:S(2)}) collective-permute-start(bf16[12,4,512]{2,1,0:T(4,128)(2,1)S(1)} %collective-permute-done.10), channel_id=1, source_target_pairs={{0,15},{1,0},{2,1},{3,2},{4,3},{5,4},{6,5},{7,6},{8,7},{9,8},{10,9... | collective-permute-start | bytes 147464 | tf_op jit(solution)/shard_map/ppermute | solution.py:27
  79.2 1.9 collective-permute-start.5
  81.8 6.7 %collective-permute-start.12 = (bf16[12,4,512]{2,1,0:T(4,128)(2,1)S(1)}, bf16[12,4,512]{2,1,0:T(4,128)(2,1)S(1)}, u32[]{:S(2)}, u32[]{:S(2)}) collective-permute-start(bf16[12,4,512]{2,1,0:T(4,128)(2,1)S(1)} %collective-permute-done.11), channel_id=1, source_target_pairs={{0,15},{1,0},{2,1},{3,2},{4,3},{5,4},{6,5},{7,6},{8,7},{9,8},{10,9... | collective-permute-start | bytes 147464 | tf_op jit(solution)/shard_map/ppermute | solution.py:27
  88.5 1.9 collective-permute-start.6
  90.6 6.7 %collective-permute-start.13 = (bf16[12,4,512]{2,1,0:T(4,128)(2,1)S(1)}, bf16[12,4,512]{2,1,0:T(4,128)(2,1)S(1)}, u32[]{:S(2)}, u32[]{:S(2)}) collective-permute-start(bf16[12,4,512]{2,1,0:T(4,128)(2,1)S(1)} %collective-permute-done.12), channel_id=1, source_target_pairs={{0,15},{1,0},{2,1},{3,2},{4,3},{5,4},{6,5},{7,6},{8,7},{9,8},{10,9... | collective-permute-start | bytes 147464 | tf_op jit(solution)/shard_map/ppermute | solution.py:27
  97.3 1.9 collective-permute-start.7
  99.2 6.7 %collective-permute-start.14 = (bf16[12,4,512]{2,1,0:T(4,128)(2,1)S(1)}, bf16[12,4,512]{2,1,0:T(4,128)(2,1)S(1)}, u32[]{:S(2)}, u32[]{:S(2)}) collective-permute-start(bf16[12,4,512]{2,1,0:T(4,128)(2,1)S(1)} %collective-permute-done.13), channel_id=1, source_target_pairs={{0,15},{1,0},{2,1},{3,2},{4,3},{5,4},{6,5},{7,6},{8,7},{9,8},{10,9... | collective-permute-start | bytes 147464 | tf_op jit(solution)/shard_map/ppermute | solution.py:27
  107.6 1.2 copy-done.2
  110.0 1.2 constant_dynamic-slice_fusion.1
  111.7 103.2 %all-to-all-done = bf16[32,1,32,2048]{3,2,1,0:T(8,128)(2,1)} async-done(((bf16[32,1,32,2048]{3,2,1,0:T(8,128)(2,1)}), bf16[32,1,32,2048]{3,2,1,0:T(8,128)(2,1)}, u32[]{:S(2)}, u32[]{:S(2)}) %all-to-all-start) | async-done | bytes 4194336 | tf_op jit(solution)/shard_map/all_to_all | solution.py:142
  215.0 2.8 gather_fusion.2
  219.6 1.4 pad_maximum_fusion
  226.3 20.7 %all-gather.1 = f32[192,4,64]{2,1,0:T(4,128)S(1)} all-gather(f32[12,4,64]{2,1,0:T(4,128)S(1)} %copy.145), channel_id=3, replica_groups=mesh['group'=32,'tensor'=16] {'tensor'}, dimensions={0}, use_global_device_ids=true | all-gather | bytes 208896 | tf_op jit(solution)/shard_map/all_gather | solution.py:36
  247.1 20.5 %all-gather = f32[192,4,64]{2,1,0:T(4,128)S(1)} all-gather(f32[12,4,64]{2,1,0:T(4,128)S(1)} %pad_maximum_fusion.2), channel_id=2, replica_groups=mesh['group'=32,'tensor'=16] {'tensor'}, dimensions={0}, use_global_device_ids=true | all-gather | bytes 208896 | tf_op jit(solution)/shard_map/all_gather | solution.py:36
  267.7 123.8 %all-gather.5.cloned.1.call-done = f32[192,4,64,128]{3,2,1,0:T(8,128)} async-done(((f32[12,4,64,128]{3,2,1,0:T(8,128)}), f32[192,4,64,128]{3,2,1,0:T(8,128)}) %all-gather.5.cloned.1.call-update) | async-done | bytes 25165840 | tf_op jit(solution)/shard_map/all_gather | solution.py:36
  391.4 1.5 slice.54
  392.9 35.1 %while.19 = (s32[]{:T(128)}, f32[12,4,64]{2,1,0:T(4,128)S(1)}, f32[12,4,64]{2,1,0:T(4,128)S(1)}, f32[12,4,64,128]{3,2,1,0:T(8,128)S(1)}, f32[16,12,4,64]{3,2,1,0...) while((s32[]{:T(128)}, f32[12,4,64]{2,1,0:T(4,128)S(1)}, ...), condition=%wide.region_10.11_spmd, body=%wide.region_9.10_spmd.sunk | while | flops 1198085 | bytes 4841623 | solution.py:41
  393.0 2.3 fusion.49
  395.4 2.3 fusion.49
  397.7 2.3 fusion.49
  400.0 2.3 fusion.49
  402.4 2.3 fusion.49
  404.7 2.3 fusion.49
  407.1 2.3 fusion.49
  409.4 2.3 fusion.49
  411.7 2.3 fusion.49
  414.1 2.3 fusion.49
  416.4 2.3 fusion.49
  418.8 2.3 fusion.49
  421.1 2.3 fusion.49
  423.5 2.3 fusion.49
  425.8 2.3 fusion.49
  432.3 1.6 fusion.8
  (147 shorter events, 18.4 us)
Async XLA Ops:
  9.3 2.5 copy-start
  14.7 17.0 %copy-start.3 = (bf16[12,4,512]{2,1,0:T(4,128)(2,1)S(1)}, bf16[12,4,512]{2,1,0:T(4,128)(2,1)}, u32[]{:S(2)}) copy-start(bf16[12,4,512]{2,1,0:T(4,128)(2,1)} %param.12) | copy-start | bytes 147460
  14.7 25.8 %copy-start.1 = (bf16[4,32,2048]{2,1,0:T(8,128)(2,1)S(1)}, bf16[4,32,2048]{2,1,0:T(8,128)(2,1)}, u32[]{:S(2)}) copy-start(bf16[4,32,2048]{2,1,0:T(8,128)(2,1)} %param.14) | copy-start | bytes 1572868
  14.7 200.2 %all-to-all-start = ((bf16[32,1,32,2048]{3,2,1,0:T(8,128)(2,1)}), bf16[32,1,32,2048]{3,2,1,0:T(8,128)(2,1)}, u32[]{:S(2)}, u32[]{:S(2)}) async-start(bf16[32,1,32,2048]{3,2,1,0:T(8,128)(2,1)} %bitcast.125), calls=%async_computation | async-start | bytes 8388608 | tf_op jit(solution)/shard_map/all_to_all | solution.py:142
  31.7 40.7 %copy-start.6 = (s32[128]{0:T(128)S(1)}, s32[128]{0:T(128)}, u32[]{:S(2)}) copy-start(s32[128]{0:T(128)} %param.16) | copy-start | bytes 1540
  31.7 359.7 %all-gather.5.cloned.1.call-start = ((), (), s32[]{:S(2)}) async-start(), calls=%async_computation.1 | async-start | bytes 26738688 | tf_op jit(solution)/shard_map/all_gather | solution.py:36
  31.8 10.6 %collective-permute-start = (bf16[12,4,512]{2,1,0:T(4,128)(2,1)S(1)}, bf16[12,4,512]{2,1,0:T(4,128)(2,1)S(1)}, u32[]{:S(2)}, u32[]{:S(2)}) collective-permute-start(bf16[12,4,512]{2,1,0:T(4,128)(2,1)S(1)} %copy-done.3), channel_id=1, source_target_pairs={{0,1},{1,2},{2,3},{3,4},{4,5},{5,6},{6,7},{7,8},{8,9},{9,10},{10,1... | collective-permute-start | bytes 147464 | tf_op jit(solution)/shard_map/ppermute | solution.py:23
  34.9 17.9 %collective-permute-start.8 = (bf16[12,4,512]{2,1,0:T(4,128)(2,1)S(1)}, bf16[12,4,512]{2,1,0:T(4,128)(2,1)S(1)}, u32[]{:S(2)}, u32[]{:S(2)}) collective-permute-start(bf16[12,4,512]{2,1,0:T(4,128)(2,1)S(1)} %copy-done.3), channel_id=1, source_target_pairs={{0,15},{1,0},{2,1},{3,2},{4,3},{5,4},{6,5},{7,6},{8,7},{9,8},{10,9... | collective-permute-start | bytes 147464 | tf_op jit(solution)/shard_map/ppermute | solution.py:27
  42.4 8.6 %collective-permute-start.1 = (bf16[12,4,512]{2,1,0:T(4,128)(2,1)S(1)}, bf16[12,4,512]{2,1,0:T(4,128)(2,1)S(1)}, u32[]{:S(2)}, u32[]{:S(2)}) collective-permute-start(bf16[12,4,512]{2,1,0:T(4,128)(2,1)S(1)} %collective-permute-done), channel_id=1, source_target_pairs={{0,1},{1,2},{2,3},{3,4},{4,5},{5,6},{6,7},{7,8},{8,9},{9,10},{10,1... | collective-permute-start | bytes 147464 | tf_op jit(solution)/shard_map/ppermute | solution.py:23
  50.9 8.6 %collective-permute-start.2 = (bf16[12,4,512]{2,1,0:T(4,128)(2,1)S(1)}, bf16[12,4,512]{2,1,0:T(4,128)(2,1)S(1)}, u32[]{:S(2)}, u32[]{:S(2)}) collective-permute-start(bf16[12,4,512]{2,1,0:T(4,128)(2,1)S(1)} %collective-permute-done.1), channel_id=1, source_target_pairs={{0,1},{1,2},{2,3},{3,4},{4,5},{5,6},{6,7},{7,8},{8,9},{9,10},{10,1... | collective-permute-start | bytes 147464 | tf_op jit(solution)/shard_map/ppermute | solution.py:23
  52.9 10.8 %collective-permute-start.9 = (bf16[12,4,512]{2,1,0:T(4,128)(2,1)S(1)}, bf16[12,4,512]{2,1,0:T(4,128)(2,1)S(1)}, u32[]{:S(2)}, u32[]{:S(2)}) collective-permute-start(bf16[12,4,512]{2,1,0:T(4,128)(2,1)S(1)} %collective-permute-done.8), channel_id=1, source_target_pairs={{0,15},{1,0},{2,1},{3,2},{4,3},{5,4},{6,5},{7,6},{8,7},{9,8},{10,9... | collective-permute-start | bytes 147464 | tf_op jit(solution)/shard_map/ppermute | solution.py:27
  59.6 10.8 %collective-permute-start.3 = (bf16[12,4,512]{2,1,0:T(4,128)(2,1)S(1)}, bf16[12,4,512]{2,1,0:T(4,128)(2,1)S(1)}, u32[]{:S(2)}, u32[]{:S(2)}) collective-permute-start(bf16[12,4,512]{2,1,0:T(4,128)(2,1)S(1)} %collective-permute-done.2), channel_id=1, source_target_pairs={{0,1},{1,2},{2,3},{3,4},{4,5},{5,6},{6,7},{7,8},{8,9},{9,10},{10,1... | collective-permute-start | bytes 147464 | tf_op jit(solution)/shard_map/ppermute | solution.py:23
  63.7 8.8 %collective-permute-start.10 = (bf16[12,4,512]{2,1,0:T(4,128)(2,1)S(1)}, bf16[12,4,512]{2,1,0:T(4,128)(2,1)S(1)}, u32[]{:S(2)}, u32[]{:S(2)}) collective-permute-start(bf16[12,4,512]{2,1,0:T(4,128)(2,1)S(1)} %collective-permute-done.9), channel_id=1, source_target_pairs={{0,15},{1,0},{2,1},{3,2},{4,3},{5,4},{6,5},{7,6},{8,7},{9,8},{10,9... | collective-permute-start | bytes 147464 | tf_op jit(solution)/shard_map/ppermute | solution.py:27
  70.4 8.8 %collective-permute-start.4 = (bf16[12,4,512]{2,1,0:T(4,128)(2,1)S(1)}, bf16[12,4,512]{2,1,0:T(4,128)(2,1)S(1)}, u32[]{:S(2)}, u32[]{:S(2)}) collective-permute-start(bf16[12,4,512]{2,1,0:T(4,128)(2,1)S(1)} %collective-permute-done.3), channel_id=1, source_target_pairs={{0,1},{1,2},{2,3},{3,4},{4,5},{5,6},{6,7},{7,8},{8,9},{9,10},{10,1... | collective-permute-start | bytes 147464 | tf_op jit(solution)/shard_map/ppermute | solution.py:23
  72.5 9.3 %collective-permute-start.11 = (bf16[12,4,512]{2,1,0:T(4,128)(2,1)S(1)}, bf16[12,4,512]{2,1,0:T(4,128)(2,1)S(1)}, u32[]{:S(2)}, u32[]{:S(2)}) collective-permute-start(bf16[12,4,512]{2,1,0:T(4,128)(2,1)S(1)} %collective-permute-done.10), channel_id=1, source_target_pairs={{0,15},{1,0},{2,1},{3,2},{4,3},{5,4},{6,5},{7,6},{8,7},{9,8},{10,9... | collective-permute-start | bytes 147464 | tf_op jit(solution)/shard_map/ppermute | solution.py:27
  79.2 9.3 %collective-permute-start.5 = (bf16[12,4,512]{2,1,0:T(4,128)(2,1)S(1)}, bf16[12,4,512]{2,1,0:T(4,128)(2,1)S(1)}, u32[]{:S(2)}, u32[]{:S(2)}) collective-permute-start(bf16[12,4,512]{2,1,0:T(4,128)(2,1)S(1)} %collective-permute-done.4), channel_id=1, source_target_pairs={{0,1},{1,2},{2,3},{3,4},{4,5},{5,6},{6,7},{7,8},{8,9},{9,10},{10,1... | collective-permute-start | bytes 147464 | tf_op jit(solution)/shard_map/ppermute | solution.py:23
  81.8 8.7 %collective-permute-start.12 = (bf16[12,4,512]{2,1,0:T(4,128)(2,1)S(1)}, bf16[12,4,512]{2,1,0:T(4,128)(2,1)S(1)}, u32[]{:S(2)}, u32[]{:S(2)}) collective-permute-start(bf16[12,4,512]{2,1,0:T(4,128)(2,1)S(1)} %collective-permute-done.11), channel_id=1, source_target_pairs={{0,15},{1,0},{2,1},{3,2},{4,3},{5,4},{6,5},{7,6},{8,7},{9,8},{10,9... | collective-permute-start | bytes 147464 | tf_op jit(solution)/shard_map/ppermute | solution.py:27
  88.5 8.7 %collective-permute-start.6 = (bf16[12,4,512]{2,1,0:T(4,128)(2,1)S(1)}, bf16[12,4,512]{2,1,0:T(4,128)(2,1)S(1)}, u32[]{:S(2)}, u32[]{:S(2)}) collective-permute-start(bf16[12,4,512]{2,1,0:T(4,128)(2,1)S(1)} %collective-permute-done.5), channel_id=1, source_target_pairs={{0,1},{1,2},{2,3},{3,4},{4,5},{5,6},{6,7},{7,8},{8,9},{9,10},{10,1... | collective-permute-start | bytes 147464 | tf_op jit(solution)/shard_map/ppermute | solution.py:23
  90.6 8.7 %collective-permute-start.13 = (bf16[12,4,512]{2,1,0:T(4,128)(2,1)S(1)}, bf16[12,4,512]{2,1,0:T(4,128)(2,1)S(1)}, u32[]{:S(2)}, u32[]{:S(2)}) collective-permute-start(bf16[12,4,512]{2,1,0:T(4,128)(2,1)S(1)} %collective-permute-done.12), channel_id=1, source_target_pairs={{0,15},{1,0},{2,1},{3,2},{4,3},{5,4},{6,5},{7,6},{8,7},{9,8},{10,9... | collective-permute-start | bytes 147464 | tf_op jit(solution)/shard_map/ppermute | solution.py:27
  97.3 8.7 %collective-permute-start.7 = (bf16[12,4,512]{2,1,0:T(4,128)(2,1)S(1)}, bf16[12,4,512]{2,1,0:T(4,128)(2,1)S(1)}, u32[]{:S(2)}, u32[]{:S(2)}) collective-permute-start(bf16[12,4,512]{2,1,0:T(4,128)(2,1)S(1)} %collective-permute-done.6), channel_id=1, source_target_pairs={{0,1},{1,2},{2,3},{3,4},{4,5},{5,6},{6,7},{7,8},{8,9},{9,10},{10,1... | collective-permute-start | bytes 147464 | tf_op jit(solution)/shard_map/ppermute | solution.py:23
  99.2 7.8 %collective-permute-start.14 = (bf16[12,4,512]{2,1,0:T(4,128)(2,1)S(1)}, bf16[12,4,512]{2,1,0:T(4,128)(2,1)S(1)}, u32[]{:S(2)}, u32[]{:S(2)}) collective-permute-start(bf16[12,4,512]{2,1,0:T(4,128)(2,1)S(1)} %collective-permute-done.13), channel_id=1, source_target_pairs={{0,15},{1,0},{2,1},{3,2},{4,3},{5,4},{6,5},{7,6},{8,7},{9,8},{10,9... | collective-permute-start | bytes 147464 | tf_op jit(solution)/shard_map/ppermute | solution.py:27
  107.6 1.2 copy-start.2
  220.9 0.9 copy-start.5
  428.3 1.9 copy-start.4
Sparse Core Ops, SparseCore 0:
  221.1 170.3 all-gather.4
